TPU v7x, 512 devices: a whole 4x8x8 slice. The times are simulated.
512 devices in a mesh: seq: 64 (over z_lo, x, y), tp: 8 (over z_hi, core).
Axes of the slice: x: 4, y: 8, z: 8 (z_hi: 4, z_lo: 2; z = z_hi * 2 + z_lo), core: 2. Of those that a mesh axis runs over, the one named last changes fastest.
Arguments:
- hidden: bfloat16 [65536, 8192], P('seq', 'tp'), may hold values from -6 to 6
- keep_first: int32 [64, 512], P('seq'), may hold values from 0 to 1023, as said below
- keep_second: int32 [16384], P('seq'), may hold values from 0 to 1023, as said below
- norm_gain: float32 [8192], replicated, may hold values from 0.1 to 1.9
- w_query: bfloat16 [8192, 4096], P('seq', 'tp'), may hold values from -1.3479223 to 1.3479223
- w_keyval: bfloat16 [8192, 2, 1024], P('seq', None, 'tp'), may hold values from -0.0508233 to 0.0508233
Outputs:
- attended: bfloat16 [16384, 4096], P('seq', 'tp')
Inputs may be any that keep to these rules, and one draw needn't show every extreme that they name: `keep_first`: each row lists 512 distinct positions in increasing order, the last being 1023. `keep_second`: each aligned run of 512 entries lists distinct positions of one merged pair in increasing order, the last being 1023.
All inputs are finite; a program needn't handle non-finite values.
Results may differ from a plain program's by a relative error of at most 0.0081.
Values may be sent and summed in bfloat16 or wider, within the bound.
A program may use at most 64 MiB of HBM per device.

v0:
```python
import math

import jax
import jax.numpy as jnp
from jax import lax
from jax.sharding import PartitionSpec as P

HD = 128


eps = 1e-05


def from_partner(block, axis, stride):
    count = lax.axis_size(axis)
    route = []
    for low in range(count):
        high = low | 1 << stride
        if high != low and high < count:
            route += [(low, high), (high, low)]
    return lax.ppermute(block, axis, route)


def rotate(values, positions):
    half_dim = values.shape[-1] // 2
    frequency = jnp.exp(
        jnp.arange(half_dim, dtype=jnp.float32) * (-2.0 * math.log(10000.0) / values.shape[-1])
    )
    angles = positions.astype(jnp.float32)[:, None] * frequency[None, :]
    cosine = jnp.cos(angles)[:, None, :]
    sine_part = jnp.sin(angles)[:, None, :]
    first_half = values[..., :half_dim]
    second_half = values[..., half_dim:]
    return jnp.concatenate(
        [
            first_half * cosine - second_half * sine_part,
            second_half * cosine + first_half * sine_part,
        ],
        axis=-1,
    )


def select_rows(chosen, source):
    one_hot = (
        chosen[:, None] == lax.broadcasted_iota(jnp.int32, (chosen.shape[0], source.shape[0]), 1)
    ).astype(source.dtype)
    return jnp.dot(one_hot, source, preferred_element_type=jnp.float32).astype(source.dtype)


def local(hidden, keep_first, keep_second, norm_gain, w_query, w_keyval):
    my_index = lax.axis_index("seq")
    is_even = my_index % 2 == 0
    own_rows = select_rows(keep_first[0], hidden)
    partner_span = from_partner(hidden, "seq", 0)
    partner_picks = from_partner(keep_first, "seq", 0)
    partner_rows = select_rows(partner_picks[0], partner_span)
    leading = jnp.where(is_even, own_rows, partner_rows)
    trailing = jnp.where(is_even, partner_rows, own_rows)
    paired = jnp.concatenate([leading, trailing], axis=0)
    quarter = select_rows(keep_second, paired)
    gathered = lax.all_gather(quarter, "tp", axis=1, tiled=True)
    widened = gathered.astype(jnp.float32)
    inv_rms = lax.rsqrt(jnp.mean(widened * widened, axis=1, keepdims=True) + eps)
    normed = (widened * inv_rms * norm_gain[None, :]).astype(jnp.bfloat16)
    row_count = normed.shape[0]
    query_cols = w_query.shape[1]
    kv_cols = w_keyval.shape[2]
    columns = normed
    query = jnp.dot(
        columns,
        lax.all_gather(w_query, "seq", axis=0, tiled=True),
        preferred_element_type=jnp.float32,
    )
    piece = lax.all_gather(w_keyval, "seq", axis=0, tiled=True)
    columns = normed
    keyval = jnp.dot(
        columns, piece.reshape(piece.shape[0], 2 * kv_cols), preferred_element_type=jnp.float32
    )
    query_heads = query_cols // HD
    kv_heads = kv_cols // HD
    positions = my_index % 4 * row_count + jnp.arange(row_count, dtype=jnp.int32)
    rot_query = rotate(query.reshape(row_count, query_heads, HD), positions).astype(jnp.bfloat16)
    keyval = keyval.reshape(row_count, 2, kv_heads, HD)
    rot_keys = rotate(keyval[:, 0], positions).astype(jnp.bfloat16)
    values = keyval[:, 1].astype(jnp.bfloat16)
    stacked = jnp.stack([rot_keys, values], axis=1)
    for bit_number in range(2):
        partner_keys = from_partner(stacked, "seq", bit_number)
        lower_half = my_index // (1 << bit_number) % 2 == 0
        stacked = jnp.where(
            lower_half,
            jnp.concatenate([stacked, partner_keys], axis=0),
            jnp.concatenate([partner_keys, stacked], axis=0),
        )
    group_size = query_heads // kv_heads
    grouped = rot_query.reshape(row_count, kv_heads, group_size, HD)
    scores = jnp.einsum(
        "qkgd,ckd->kgqc", grouped, stacked[:, 0], preferred_element_type=jnp.float32
    ) / math.sqrt(HD)
    causal = positions[:, None] >= jnp.arange(stacked.shape[0], dtype=jnp.int32)[None, :]
    scores = jnp.where(causal, scores, -jnp.inf)
    row_max = jnp.max(scores, axis=-1, keepdims=True)
    weights = jnp.exp(scores - row_max)
    weights = (weights / jnp.sum(weights, axis=-1, keepdims=True)).astype(jnp.bfloat16)
    result = jnp.einsum(
        "kgqc,ckd->qkgd", weights, stacked[:, 1], preferred_element_type=jnp.float32
    )
    return result.reshape(row_count, query_heads * HD).astype(jnp.bfloat16)


def solution(mesh):
    placed = (P("seq", "tp"), P("seq", None), P("seq"), P(), P("seq", "tp"), P("seq", None, "tp"))
    return jax.shard_map(
        local, mesh=mesh, in_specs=placed, out_specs=P("seq", "tp"), check_vma=False
    )
```

profile of v0, /device:TPU:128, one launch (start us, length us, event | category | flops | bytes accessed | tf_op | source)
XLA Modules:
  0.0 710.5 jit_solution(9385975159975554096)
XLA Ops:
  6.5 0.7 all-gather.6.cloned.1.call-update
  7.3 3.5 collective-permute-start.1
  10.8 2.4 collective-permute-start
  13.2 2.9 fusion.17
  16.1 46.4 %collective-permute-done = s32[1,512]{1,0:T(1,128)S(1)} collective-permute-done((s32[1,512]{1,0:T(1,128)}, s32[1,512]{1,0:T(1,128)S(1)}, u32[]{:S(2)}, u32[]{:S(2)}) %collective-permute-start) | collective-permute-done | bytes 2080 | tf_op jit(solution)/shard_map/ppermute | solution.py:21
  62.5 1.3 broadcast_select_fusion.1
  63.9 1.6 fusion.18
  65.5 0.7 all-gather.8.cloned.1.call-update
  66.2 252.9 %all-gather.6.cloned.1.call-done = bf16[8192,2,128]{2,1,0:T(2,128)(2,1)} async-done(((bf16[128,2,128]{2,1,0:T(2,128)(2,1)}), bf16[8192,2,128]{2,1,0:T(2,128)(2,1)}) %all-gather.6.cloned.1.call-update) | async-done | bytes 4194320 | tf_op jit(solution)/shard_map/all_gather | solution.py:74
  319.2 11.2 %copy.25 = bf16[8192,2,128]{0,2,1:T(8,128)(2,1)} copy(bf16[8192,2,128]{2,1,0:T(2,128)(2,1)} %all-gather.6.cloned.1.call-done) | data formatting | bytes 8388608 | tf_op jit(solution)/shard_map/reshape | solution.py:77
  330.4 43.9 %all-gather.4.cloned.1.call-done = bf16[256,8192]{1,0:T(8,128)(2,1)} async-done(((bf16[256,1024]{1,0:T(8,128)(2,1)}), bf16[256,8192]{1,0:T(8,128)(2,1)}) %all-gather.4.cloned.1.call-update) | async-done | bytes 4194320 | tf_op jit(solution)/shard_map/all_gather | solution.py:61
  374.3 3.3 fusion
  377.5 0.2 copy-done
  377.7 3.8 fusion.3
  381.6 0.3 fusion.44
  381.9 3.4 collective-permute-start.2
  385.3 0.5 multiply_cosine_fusion
  385.9 3.5 collective-permute-done.2
  389.6 4.5 collective-permute-start.3
  394.1 0.2 iota_compare_fusion.8
  394.3 0.1 fusion.31
  394.4 16.5 %collective-permute-done.3 = bf16[512,2,1,128]{0,3,1,2:T(8,128)(2,1)S(1)} collective-permute-done((bf16[512,2,1,128]{0,3,1,2:T(8,128)(2,1)S(1)}, bf16[512,2,1,128]{0,3,1,2:T(8,128)(2,1)S(1)}, u32[]{:S(2)}, u32[]{:S(2)}) %collective-permute-start.3) | collective-permute-done | bytes 262176 | tf_op jit(solution)/shard_map/ppermute | solution.py:21
  410.9 0.1 maximum_select_fusion
  411.0 281.1 %all-gather.8.cloned.1.call-done = bf16[8192,512]{1,0:T(8,128)(2,1)} async-done(((bf16[128,512]{1,0:T(8,128)(2,1)}), bf16[8192,512]{1,0:T(8,128)(2,1)}) %all-gather.8.cloned.1.call-update) | async-done | bytes 8388624 | tf_op jit(solution)/shard_map/all_gather | solution.py:71
  692.1 7.0 fusion.24
  699.2 0.2 reshape.381
  699.4 0.3 fusion.51
  699.7 0.1 subtract_convert_fusion
  699.9 1.0 fusion.7
  700.8 0.9 fusion.6
  701.8 1.3 fusion.21
  703.1 0.8 copy.22
  (18 shorter events, 0.3 us)
Async XLA Ops:
  6.5 312.6 %all-gather.6.cloned.1.call-start = ((), (), s32[]{:S(2)}) async-start(), calls=%async_computation.1 | async-start | bytes 4259840 | tf_op jit(solution)/shard_map/all_gather | solution.py:74
  7.3 367.0 %all-gather.4.cloned.1.call-start = ((), (), s32[]{:S(2)}) async-start(), calls=%async_computation | async-start | bytes 4718592 | tf_op jit(solution)/shard_map/all_gather | solution.py:61
  7.3 55.2 %collective-permute-start.1 = (bf16[1024,1024]{1,0:T(8,128)(2,1)}, bf16[1024,1024]{1,0:T(8,128)(2,1)S(1)}, u32[]{:S(2)}, u32[]{:S(2)}) collective-permute-start(bf16[1024,1024]{1,0:T(8,128)(2,1)} %param.6), channel_id=1, source_target_pairs={{0,8},{8,0},{16,24},{24,16},{32,40},{40,32},{48,56},{56,48},{64,72... | collective-permute-start | bytes 6291464 | tf_op jit(solution)/shard_map/ppermute | solution.py:21
  10.8 51.7 %collective-permute-start = (s32[1,512]{1,0:T(1,128)}, s32[1,512]{1,0:T(1,128)S(1)}, u32[]{:S(2)}, u32[]{:S(2)}) collective-permute-start(s32[1,512]{1,0:T(1,128)} %param.7), channel_id=1, source_target_pairs={{0,8},{8,0},{16,24},{24,16},{32,40},{40,32},{48,56},{56,48},{64,72... | collective-permute-start | bytes 6152 | tf_op jit(solution)/shard_map/ppermute | solution.py:21
  62.5 1.3 copy-start.2
  65.5 626.7 %all-gather.8.cloned.1.call-start = ((), (), s32[]{:S(2)}) async-start(), calls=%async_computation.2 | async-start | bytes 8519680 | tf_op jit(solution)/shard_map/all_gather | solution.py:71
  319.2 58.4 %copy-start.1 = (f32[8192]{0:T(1024)S(1)}, f32[8192]{0:T(1024)}, u32[]{:S(2)}) copy-start(f32[8192]{0:T(1024)} %param.9) | copy-start | bytes 98308
  374.3 3.4 copy-start
  381.9 7.5 %collective-permute-start.2 = (bf16[256,2,1,128]{0,3,1,2:T(8,128)(2,1)S(1)}, bf16[256,2,1,128]{0,3,1,2:T(8,128)(2,1)S(1)}, u32[]{:S(2)}, u32[]{:S(2)}) collective-permute-start(bf16[256,2,1,128]{0,3,1,2:T(8,128)(2,1)S(1)} %get-tuple-element.14), channel_id=1, source_target_pairs={{0,8},{8,0},{16,24},{24,16},{32,40},{40,32},{48,56},{56,48},{64,72... | collective-permute-start | bytes 393224 | tf_op jit(solution)/shard_map/ppermute | solution.py:21
  389.6 21.3 %collective-permute-start.3 = (bf16[512,2,1,128]{0,3,1,2:T(8,128)(2,1)S(1)}, bf16[512,2,1,128]{0,3,1,2:T(8,128)(2,1)S(1)}, u32[]{:S(2)}, u32[]{:S(2)}) collective-permute-start(bf16[512,2,1,128]{0,3,1,2:T(8,128)(2,1)S(1)} %maximum_select_fusion.2), channel_id=1, source_target_pairs={{0,16},{16,0},{8,24},{24,8},{32,48},{48,32},{40,56},{56,40},{64,80... | collective-permute-start | bytes 786440 | tf_op jit(solution)/shard_map/ppermute | solution.py:21
Sparse Core Ops, SparseCore 0:
  9.4 309.6 all-gather.5
  321.3 52.9 all-gather.3
  376.4 315.7 all-gather.7
where the time goes:
time: 711 us; the launch traced here: 710 us
  waiting for transfers between devices  646 us (91%)
  matrix products  18.9 us (3%)
  starting transfers between devices  13.8 us (2%)
  between operations  13.4 us (2%)
  local copies, waits for them, and re-layouts  12.8 us (2%)
    all_gather x1, waiting for transfers between devices, local(): lax.all_gather(w_query, 'seq', axis=0, tiled=True)  281 us
    all_gather x1, waiting for transfers between devices, local(): piece = lax.all_gather(w_keyval, 'seq', axis=0, tiled=True)  253 us
    ppermute x4, waiting for transfers between devices, from_partner(): return lax.ppermute(block, axis, route)  66.5 us
    all_gather x1, waiting for transfers between devices, local(): gathered = lax.all_gather(quarter, 'tp', axis=1, tiled=True)  43.9 us
  transfers between devices with their start and end apart: 7, of which 6 were waited for; matrix products, arithmetic and copies ran while one was open for 4% of the time, Pallas kernels for 0%

commit v1 on v0

--- a/solution.py
+++ b/solution.py
@@ -3,10 +3,14 @@
 import jax
 import jax.numpy as jnp
 from jax import lax
+from jax.experimental import pallas as pl
+from jax.experimental.pallas import tpu as pltpu
 from jax.sharding import PartitionSpec as P
 
 HD = 128
-
+NX, NY = 4, 8
+MESH = pl.DeviceIdType.MESH
+X_RIGHT, X_LEFT, Y_RIGHT, Y_LEFT, Z_OTHER = (1, 0, 0), (-1, 0, 0), (0, 1, 0), (0, -1, 0), (0, 0, 1)
 
 eps = 1e-05
 
@@ -19,6 +23,175 @@
         if high != low and high < count:
             route += [(low, high), (high, low)]
     return lax.ppermute(block, axis, route)
+
+
+def gather_weights(wq_ref, wkv_ref, q_all, kv_all, send_sems, recv_sems, local_sems):
+    me = lax.axis_index("seq")
+    tp = lax.axis_index("tp")
+    zl, x, y = me // (NX * NY), me // NY % NX, me % NY
+
+    def device(way):
+        dx, dy, dz = way
+        nx, ny, nz = lax.rem(x + dx + NX, NX), lax.rem(y + dy + NY, NY), lax.rem(zl + dz, 2)
+        return (nz * (NX * NY) + nx * NY + ny, tp)
+
+    def at(ref, other, xo, yo):
+        plane = lax.rem(zl + other, 2)
+        row = lax.rem(y + yo + 2 * NY, NY)
+        if xo is None:
+            return ref.at[plane, :, row]
+        return ref.at[plane, lax.rem(x + xo + 2 * NX, NX), row]
+
+    barrier = pltpu.get_barrier_semaphore()
+    for way in (X_RIGHT, X_LEFT, Y_RIGHT, Y_LEFT, Z_OTHER):
+        pl.semaphore_signal(barrier, inc=1, device_id=device(way), device_id_type=MESH)
+    pl.semaphore_wait(barrier, 5)
+
+    mine_q = pltpu.make_async_copy(wq_ref, at(q_all, 0, 0, 0), local_sems.at[0])
+    mine_kv = pltpu.make_async_copy(wkv_ref, at(kv_all, 0, 0, 0), local_sems.at[1])
+    mine_q.start()
+    mine_kv.start()
+
+    copies = []
+    table = {}
+
+    def send(ref, way, other, xo, yo, src=None):
+        number = len(copies)
+        dst = at(ref, other, xo, yo)
+        copy = pltpu.make_async_remote_copy(
+            src_ref=dst if src is None else src,
+            dst_ref=dst,
+            send_sem=send_sems.at[number],
+            recv_sem=recv_sems.at[number],
+            device_id=device(way),
+            device_id_type=MESH,
+        )
+        copy.start()
+        copies.append(copy)
+        dx, dy, dz = way
+        there = (other + dz) % 2, None if xo is None else xo - dx, yo - dy
+        landing = at(ref, *there)
+        table[(id(ref), way) + there] = pltpu.make_async_remote_copy(
+            src_ref=landing,
+            dst_ref=landing,
+            send_sem=send_sems.at[number],
+            recv_sem=recv_sems.at[number],
+            device_id=device(way),
+            device_id_type=MESH,
+        )
+
+    def arrived(ref, way, other, xo, yo):
+        table.pop((id(ref), way, other, xo, yo)).wait_recv()
+
+    send(kv_all, Z_OTHER, 0, 0, 0, wkv_ref)
+    send(q_all, Z_OTHER, 0, 0, 0, wq_ref)
+    for way in (X_RIGHT, X_LEFT):
+        send(kv_all, way, 0, 0, 0, wkv_ref)
+    for way in (Y_RIGHT, Y_LEFT):
+        send(q_all, way, 0, 0, 0, wq_ref)
+    for way in (X_RIGHT, X_LEFT):
+        send(q_all, way, 0, 0, 0, wq_ref)
+    arrived(kv_all, Z_OTHER, 1, 0, 0)
+    for way in (X_RIGHT, X_LEFT):
+        send(kv_all, way, 1, 0, 0)
+    arrived(q_all, Z_OTHER, 1, 0, 0)
+    for way in (Y_RIGHT, Y_LEFT):
+        send(q_all, way, 1, 0, 0)
+    for way in (X_RIGHT, X_LEFT):
+        send(q_all, way, 1, 0, 0)
+    arrived(kv_all, X_RIGHT, 0, -1, 0)
+    send(kv_all, X_RIGHT, 0, -1, 0)
+    arrived(kv_all, X_LEFT, 1, 1, 0)
+    send(kv_all, X_LEFT, 1, 1, 0)
+    arrived(kv_all, X_LEFT, 0, 1, 0)
+    arrived(kv_all, X_RIGHT, 1, -1, 0)
+    mine_kv.wait()
+
+    pending = [0]
+
+    def second_hop(yo):
+        arrived(q_all, X_RIGHT, 0, -1, yo)
+        send(q_all, X_RIGHT, 0, -1, yo)
+        arrived(q_all, X_LEFT, 1, 1, yo)
+        send(q_all, X_LEFT, 1, 1, yo)
+
+    def kv_hop(step):
+        if step == 0:
+            arrived(kv_all, X_RIGHT, 0, -2, 0)
+            arrived(kv_all, X_LEFT, 1, 2, 0)
+            for way in (Y_RIGHT, Y_LEFT):
+                for other in (0, 1):
+                    send(kv_all, way, other, None, 0)
+            return
+        for other in (0, 1):
+            for way, sign, far in ((Y_RIGHT, -1, 4 - other), (Y_LEFT, 1, 3 + other)):
+                if step <= far:
+                    arrived(kv_all, way, other, None, sign * step)
+                    if step < far:
+                        send(kv_all, way, other, None, sign * step)
+
+    def q_hop(step):
+        for other in (0, 1):
+            for way, sign, far in ((Y_RIGHT, -1, 4 - other), (Y_LEFT, 1, 3 + other)):
+                if step <= far:
+                    arrived(q_all, way, other, 0, sign * step)
+                    if step < far:
+                        send(q_all, way, other, 0, sign * step)
+                    for side in (X_RIGHT, X_LEFT):
+                        send(q_all, side, other, 0, sign * step)
+
+    q_hop(1)
+    kv_hop(0)
+    second_hop(0)
+    q_hop(2)
+    second_hop(-1)
+    second_hop(1)
+    kv_hop(1)
+    q_hop(3)
+    second_hop(-2)
+    kv_hop(2)
+    second_hop(2)
+    for other, way, sign in ((0, Y_RIGHT, -1), (1, Y_LEFT, 1)):
+        arrived(q_all, way, other, 0, sign * 4)
+        for side in (X_RIGHT, X_LEFT):
+            send(q_all, side, other, 0, sign * 4)
+    second_hop(-3)
+    kv_hop(3)
+    second_hop(3)
+    arrived(q_all, X_RIGHT, 0, -1, -4)
+    send(q_all, X_RIGHT, 0, -1, -4)
+    arrived(q_all, X_LEFT, 1, 1, 4)
+    send(q_all, X_LEFT, 1, 1, 4)
+    kv_hop(4)
+    for rest in list(table.values()):
+        rest.wait_recv()
+    mine_q.wait()
+    for copy in copies:
+        copy.wait_send()
+
+
+COPIES = 84
+
+
+def all_weights(w_query, w_keyval):
+    rows, qc = w_query.shape
+    kc = w_keyval.shape[1]
+    return pl.pallas_call(
+        gather_weights,
+        out_shape=(
+            jax.ShapeDtypeStruct((2, NX, NY, rows, qc), jnp.bfloat16),
+            jax.ShapeDtypeStruct((2, NX, NY, rows, kc), jnp.bfloat16),
+        ),
+        in_specs=[pl.BlockSpec(memory_space=pl.ANY)] * 2,
+        out_specs=(pl.BlockSpec(memory_space=pl.ANY),) * 2,
+        scratch_shapes=[
+            pltpu.SemaphoreType.DMA((COPIES,)),
+            pltpu.SemaphoreType.DMA((COPIES,)),
+            pltpu.SemaphoreType.DMA((2,)),
+        ],
+        compiler_params=pltpu.CompilerParams(collective_id=0, has_side_effects=True),
+        cost_estimate=pl.CostEstimate(flops=0, bytes_accessed=200_000_000, transcendentals=0),
+    )(w_query, w_keyval)
 
 
 def rotate(values, positions):
@@ -49,33 +222,24 @@
 
 def local(hidden, keep_first, keep_second, norm_gain, w_query, w_keyval):
     my_index = lax.axis_index("seq")
-    is_even = my_index % 2 == 0
-    own_rows = select_rows(keep_first[0], hidden)
-    partner_span = from_partner(hidden, "seq", 0)
-    partner_picks = from_partner(keep_first, "seq", 0)
-    partner_rows = select_rows(partner_picks[0], partner_span)
-    leading = jnp.where(is_even, own_rows, partner_rows)
-    trailing = jnp.where(is_even, partner_rows, own_rows)
-    paired = jnp.concatenate([leading, trailing], axis=0)
-    quarter = select_rows(keep_second, paired)
+    odd = my_index % 2
+    row_count = keep_second.shape[0]
+    kept = keep_first.shape[1]
+    query_cols = w_query.shape[1]
+    kv_cols = w_keyval.shape[2]
+    q_all, kv_all = all_weights(w_query, w_keyval.reshape(-1, 2 * kv_cols))
+
+    other_picks = from_partner(keep_second, "seq", 0)
+    own_kept = select_rows(keep_first[0], hidden)
+    own_part = select_rows(keep_second - odd * kept, own_kept)
+    other_part = select_rows(other_picks - odd * kept, own_kept)
+    quarter = own_part + from_partner(other_part, "seq", 0)
     gathered = lax.all_gather(quarter, "tp", axis=1, tiled=True)
     widened = gathered.astype(jnp.float32)
     inv_rms = lax.rsqrt(jnp.mean(widened * widened, axis=1, keepdims=True) + eps)
     normed = (widened * inv_rms * norm_gain[None, :]).astype(jnp.bfloat16)
-    row_count = normed.shape[0]
-    query_cols = w_query.shape[1]
-    kv_cols = w_keyval.shape[2]
-    columns = normed
-    query = jnp.dot(
-        columns,
-        lax.all_gather(w_query, "seq", axis=0, tiled=True),
-        preferred_element_type=jnp.float32,
-    )
-    piece = lax.all_gather(w_keyval, "seq", axis=0, tiled=True)
-    columns = normed
-    keyval = jnp.dot(
-        columns, piece.reshape(piece.shape[0], 2 * kv_cols), preferred_element_type=jnp.float32
-    )
+    query = jnp.dot(normed, q_all.reshape(-1, query_cols), preferred_element_type=jnp.float32)
+    keyval = jnp.dot(normed, kv_all.reshape(-1, 2 * kv_cols), preferred_element_type=jnp.float32)
     query_heads = query_cols // HD
     kv_heads = kv_cols // HD
     positions = my_index % 4 * row_count + jnp.arange(row_count, dtype=jnp.int32)

time: 711 us -> 169 us (0.24)
  the two profiles are of different devices: /device:TPU:128 before, /device:TPU:256 now
where the time goes in v1:
time: 169 us; the launch traced here: 168 us
  Pallas kernels  79.8 us (47%)
  waiting for transfers between devices  24 us (14%)
  local copies, waits for them, and re-layouts  19.4 us (11%)
  between operations  13.7 us (8%)
  matrix products  12.8 us (8%)
  starting transfers between devices  12 us (7%)
  other arithmetic  6.49 us (4%)
    pallas_call x1, Pallas kernels, all_weights(): pl.pallas_call(gather_weights, out_shape=(jax.ShapeDtypeStruct((2, NX, NY...  79.8 us
    ppermute x4, waiting for transfers between devices, from_partner(): return lax.ppermute(block, axis, route)  24 us
    ppermute x4, starting transfers between devices, from_partner(): return lax.ppermute(block, axis, route)  12 us
    dot_general x1, local copies, waits for them, and re-layouts, local(): jnp.dot(normed, q_all.reshape(-1, query_cols), preferred_element_type=jnp...  11.5 us
    dot_general x1, local copies, waits for them, and re-layouts, local(): jnp.dot(normed, kv_all.reshape(-1, 2 * kv_cols), preferred_element_type=j...  6.37 us
    dot_general x1, matrix products, local(): jnp.dot(normed, kv_all.reshape(-1, 2 * kv_cols), preferred_element_type=j...  5.22 us
  transfers between devices with their start and end apart: 5, of which 4 were waited for; matrix products, arithmetic and copies ran while one was open for 14% of the time, Pallas kernels for 47%

profile of v1, /device:TPU:256, one launch (start us, length us, event | category | flops | bytes accessed | tf_op | source)
XLA Modules:
  0.0 168.3 jit_solution(7621287626540883862)
XLA Ops:
  6.5 3.6 %collective-permute-start = (s32[256]{0:T(256)}, s32[256]{0:T(256)S(1)}, u32[]{:S(2)}, u32[]{:S(2)}) collective-permute-start(s32[256]{0:T(256)} %param.8), channel_id=1, source_target_pairs={{0,8},{8,0},{16,24},{24,16},{32,40},{40,32},{48,56},{56,48},{64,72... | collective-permute-start | bytes 3080 | tf_op jit(solution)/shard_map/ppermute | solution.py:25
  10.2 2.0 %fusion.13 = bf16[512,1024]{1,0:T(8,128)(2,1)S(1)} fusion(bf16[1024,1024]{1,0:T(8,128)(2,1)S(1)} %copy-done, s32[512]{0:T(512)} %bitcast.87), kind=kOutput, calls=%fused_computation.17 | convolution fusion | flops 1074790400 | bytes 3147776 | tf_op jit(solution)/shard_map/dot_general | solution.py:220
  12.2 0.1 collective-permute-done
  12.3 0.5 convolution_convert_fusion
  12.8 3.5 %collective-permute-start.1 = (bf16[256,1024]{1,0:T(8,128)(2,1)S(1)}, bf16[256,1024]{1,0:T(8,128)(2,1)S(1)}, u32[]{:S(2)}, u32[]{:S(2)}) collective-permute-start(bf16[256,1024]{1,0:T(8,128)(2,1)S(1)} %convolution_convert_fusion), channel_id=1, source_target_pairs={{0,8},{8,0},{16,24},{24,16},{32,40},{40,32},{48,56},{56,48},{64,72... | collective-permute-start | bytes 1572872 | tf_op jit(solution)/shard_map/ppermute | solution.py:25
  16.3 0.5 convolution_convert_fusion.1
  16.8 11.1 %collective-permute-done.1 = bf16[256,1024]{1,0:T(8,128)(2,1)S(1)} collective-permute-done((bf16[256,1024]{1,0:T(8,128)(2,1)S(1)}, bf16[256,1024]{1,0:T(8,128)(2,1)S(1)}, u32[]{:S(2)}, u32[]{:S(2)}) %collective-permute-start.1) | collective-permute-done | bytes 524320 | tf_op jit(solution)/shard_map/ppermute | solution.py:25
  28.0 1.0 add.48
  29.0 0.0 all-gather.2.cloned.1.call-update
  29.1 0.6 copy.21
  29.7 79.8 %shard_map.64 = (bf16[2,4,8,128,512]{4,3,2,1,0:T(8,128)(2,1)}, bf16[2,4,8,128,256]{4,3,2,1,0:T(8,128)(2,1)}) custom-call(bf16[128,512]{1,0:T(8,128)(2,1)} %wq_ref.1, bf16[128,256]{1,0:T(8,128)(2,1)} %bitcast.82), custom_call_target="tpu_custom_call" | custom-call | bytes 200000000 | tf_op jit(solution)/shard_map/pallas_call | solution.py:179
  109.5 11.5 %copy.10 = bf16[512,8192]{1,0:T(8,128)(2,1)} copy(bf16[512,8192]{0,1:T(8,128)(2,1)} %bitcast.78) | data formatting | bytes 16777216 | tf_op jit(solution)/shard_map/dot_general | solution.py:241
  121.0 6.4 %copy.7 = bf16[256,8192]{1,0:T(8,128)(2,1)} copy(bf16[256,8192]{0,1:T(8,128)(2,1)} %bitcast.80) | data formatting | bytes 8388608 | tf_op jit(solution)/shard_map/dot_general | solution.py:242
  127.5 0.3 multiply_cosine_fusion
  127.8 0.2 iota_compare_fusion.4
  127.9 0.0 all-gather.2.cloned.1.call-done
  128.0 3.3 %fusion = f32[256]{0:T(256)S(1)} fusion(bf16[256,8192]{1,0:T(8,128)(2,1)} %all-gather.2.cloned.1.call-done), kind=kLoop, calls=%fused_computation.2 | loop fusion | flops 6291200 | bytes 4195328 | tf_op jit(solution)/shard_map/reduce_sum | solution.py:239
  131.3 5.2 %fusion.8 = f32[256,2,128]{0,2,1:T(8,128)S(1)} fusion(bf16[2,128,8192]{2,1,0:T(8,128)(2,1)} %bitcast.79, bf16[256,8192]{1,0:T(8,128)(2,1)} %all-gather.2.cloned.1.call-done, f32[8192]{0:T(1024)S(1)} %copy-done.4, f32[256]{0:T(256)S(1)} %add_rsqrt_fusion), kind=kOutput, calls=%fused_computation.12 | convolution fusion | flops 1082130432 | bytes 8684544 | tf_op jit(solution)/shard_map/dot_general | solution.py:242
  136.5 0.3 fusion.34
  136.9 1.9 %collective-permute-start.2 = (bf16[256,2,1,128]{0,3,1,2:T(8,128)(2,1)S(1)}, bf16[256,2,1,128]{0,3,1,2:T(8,128)(2,1)S(1)}, u32[]{:S(2)}, u32[]{:S(2)}) collective-permute-start(bf16[256,2,1,128]{0,3,1,2:T(8,128)(2,1)S(1)} %get-tuple-element.14), channel_id=1, source_target_pairs={{0,8},{8,0},{16,24},{24,16},{32,40},{40,32},{48,56},{56,48},{64,72... | collective-permute-start | bytes 393224 | tf_op jit(solution)/shard_map/ppermute | solution.py:25
  138.9 2.5 %fusion.6 = f32[256,4,128]{0,2,1:T(8,128)S(1)} fusion(bf16[4,128,8192]{2,1,0:T(8,128)(2,1)S(1)} %bitcast.77, bf16[256,8192]{1,0:T(8,128)(2,1)S(1)} %copy-done.1, f32[8192]{0:T(1024)S(1)} %copy-done.4, f32[256]{0:T(256)S(1)} %add_rsqrt_fusion), kind=kOutput, calls=%fused_computation.11 | convolution fusion | flops 2155872256 | bytes 13140992 | tf_op jit(solution)/shard_map/dot_general | solution.py:241
  141.3 2.4 %collective-permute-done.2 = bf16[256,2,1,128]{0,3,1,2:T(8,128)(2,1)S(1)} collective-permute-done((bf16[256,2,1,128]{0,3,1,2:T(8,128)(2,1)S(1)}, bf16[256,2,1,128]{0,3,1,2:T(8,128)(2,1)S(1)}, u32[]{:S(2)}, u32[]{:S(2)}) %collective-permute-start.2) | collective-permute-done | bytes 131104 | tf_op jit(solution)/shard_map/ppermute | solution.py:25
  143.8 0.1 maximum_select_fusion.2
  143.9 3.0 %collective-permute-start.3 = (bf16[512,2,1,128]{0,3,1,2:T(8,128)(2,1)S(1)}, bf16[512,2,1,128]{0,3,1,2:T(8,128)(2,1)S(1)}, u32[]{:S(2)}, u32[]{:S(2)}) collective-permute-start(bf16[512,2,1,128]{0,3,1,2:T(8,128)(2,1)S(1)} %maximum_select_fusion.2), channel_id=1, source_target_pairs={{0,16},{16,0},{8,24},{24,8},{32,48},{48,32},{40,56},{56,40},{64,80... | collective-permute-start | bytes 786440 | tf_op jit(solution)/shard_map/ppermute | solution.py:25
  146.9 0.1 subtract_convert_fusion
  146.9 0.1 fusion.19
  147.1 10.3 %collective-permute-done.3 = bf16[512,2,1,128]{0,3,1,2:T(8,128)(2,1)S(1)} collective-permute-done((bf16[512,2,1,128]{0,3,1,2:T(8,128)(2,1)S(1)}, bf16[512,2,1,128]{0,3,1,2:T(8,128)(2,1)S(1)}, u32[]{:S(2)}, u32[]{:S(2)}) %collective-permute-start.3) | collective-permute-done | bytes 262176 | tf_op jit(solution)/shard_map/ppermute | solution.py:25
  157.4 0.1 maximum_select_fusion
  157.5 0.9 fusion.5
  158.4 0.9 fusion.4
  159.3 1.3 fusion.14
  160.6 0.8 copy.14
  (25 shorter events, 0.1 us)
Async XLA Ops:
  6.5 3.6 %copy-start = (bf16[1024,1024]{1,0:T(8,128)(2,1)S(1)}, bf16[1024,1024]{1,0:T(8,128)(2,1)}, u32[]{:S(2)}) copy-start(bf16[1024,1024]{1,0:T(8,128)(2,1)} %param.6) | copy-start | bytes 6291460
  6.5 121.4 %all-gather.2.cloned.1.call-start = ((), (), s32[]{:S(2)}) async-start(), calls=%async_computation | async-start | bytes 4718592 | tf_op jit(solution)/shard_map/all_gather | solution.py:237
  6.5 5.8 %collective-permute-start = (s32[256]{0:T(256)}, s32[256]{0:T(256)S(1)}, u32[]{:S(2)}, u32[]{:S(2)}) collective-permute-start(s32[256]{0:T(256)} %param.8), channel_id=1, source_target_pairs={{0,8},{8,0},{16,24},{24,16},{32,40},{40,32},{48,56},{56,48},{64,72... | collective-permute-start | bytes 3080 | tf_op jit(solution)/shard_map/ppermute | solution.py:25
  10.2 6.2 %copy-start.3 = (s32[256]{0:T(256)S(1)}, s32[256]{0:T(256)}, u32[]{:S(2)}) copy-start(s32[256]{0:T(256)} %param.8) | copy-start | bytes 3076
  12.2 16.9 %copy-start.2 = (bf16[128,2,128]{2,1,0:T(2,128)(2,1)S(1)}, bf16[128,2,128]{2,1,0:T(2,128)(2,1)}, u32[]{:S(2)}) copy-start(bf16[128,2,128]{2,1,0:T(2,128)(2,1)} %param.11) | copy-start | bytes 196612
  12.8 15.1 %collective-permute-start.1 = (bf16[256,1024]{1,0:T(8,128)(2,1)S(1)}, bf16[256,1024]{1,0:T(8,128)(2,1)S(1)}, u32[]{:S(2)}, u32[]{:S(2)}) collective-permute-start(bf16[256,1024]{1,0:T(8,128)(2,1)S(1)} %convolution_convert_fusion), channel_id=1, source_target_pairs={{0,8},{8,0},{16,24},{24,16},{32,40},{40,32},{48,56},{56,48},{64,72... | collective-permute-start | bytes 1572872 | tf_op jit(solution)/shard_map/ppermute | solution.py:25
  127.4 3.8 %copy-start.4 = (f32[8192]{0:T(1024)S(1)}, f32[8192]{0:T(1024)}, u32[]{:S(2)}) copy-start(f32[8192]{0:T(1024)} %param.9) | copy-start | bytes 98308
  128.0 10.9 %slice-start = ((s8[8388608]{0:T(1024)(128)(4,1)}), s8[4194304]{0:T(1024)(128)(4,1)S(1)}, s32[]{:S(2)}) async-start(s8[8388608]{0:T(1024)(128)(4,1)} %bitcast.75), calls=%async_computation.1 | async-start | bytes 8388608
  131.3 7.6 %slice-start.1 = ((s8[8388608]{0:T(1024)(128)(4,1)}), s8[4194304]{0:T(1024)(128)(4,1)S(1)}, s32[]{:S(2)}) async-start(s8[8388608]{0:T(1024)(128)(4,1)} %bitcast.75), calls=%async_computation.2 | async-start | bytes 8388608
  131.3 7.6 %copy-start.1 = (bf16[256,8192]{1,0:T(8,128)(2,1)S(1)}, bf16[256,8192]{1,0:T(8,128)(2,1)}, u32[]{:S(2)}) copy-start(bf16[256,8192]{1,0:T(8,128)(2,1)} %all-gather.2.cloned.1.call-done) | copy-start | bytes 12582916
  136.9 6.9 %collective-permute-start.2 = (bf16[256,2,1,128]{0,3,1,2:T(8,128)(2,1)S(1)}, bf16[256,2,1,128]{0,3,1,2:T(8,128)(2,1)S(1)}, u32[]{:S(2)}, u32[]{:S(2)}) collective-permute-start(bf16[256,2,1,128]{0,3,1,2:T(8,128)(2,1)S(1)} %get-tuple-element.14), channel_id=1, source_target_pairs={{0,8},{8,0},{16,24},{24,16},{32,40},{40,32},{48,56},{56,48},{64,72... | collective-permute-start | bytes 393224 | tf_op jit(solution)/shard_map/ppermute | solution.py:25
  143.9 13.5 %collective-permute-start.3 = (bf16[512,2,1,128]{0,3,1,2:T(8,128)(2,1)S(1)}, bf16[512,2,1,128]{0,3,1,2:T(8,128)(2,1)S(1)}, u32[]{:S(2)}, u32[]{:S(2)}) collective-permute-start(bf16[512,2,1,128]{0,3,1,2:T(8,128)(2,1)S(1)} %maximum_select_fusion.2), channel_id=1, source_target_pairs={{0,16},{16,0},{8,24},{24,8},{32,48},{48,32},{40,56},{56,40},{64,80... | collective-permute-start | bytes 786440 | tf_op jit(solution)/shard_map/ppermute | solution.py:25
Sparse Core Ops, SparseCore 0:
  29.1 53.7 all-gather.1

commit v2 on v1

v2 whole, which is shorter than its diff:
```python
import functools
import math

import jax
import jax.numpy as jnp
import numpy as np
from jax import lax
from jax.experimental import pallas as pl
from jax.experimental.pallas import tpu as pltpu
from jax.sharding import PartitionSpec as P

HD = 128
NX, NY, NZ = 4, 8, 4
LINE = 4
NT = 2 * NZ
MESH = pl.DeviceIdType.MESH
X_RIGHT, X_LEFT, Y_RIGHT, Y_LEFT, Z_OTHER = (1, 0, 0), (-1, 0, 0), (0, 1, 0), (0, -1, 0), (0, 0, 1)
COPIES = 97
BF16, F32 = jnp.bfloat16, jnp.float32

eps = 1e-05


def one_hot(picks, first, count):
    n = picks.shape[1]
    down = jnp.transpose(jnp.broadcast_to(picks, (128, n))) - first
    lane = lax.broadcasted_iota(jnp.int32, (n, 128), 1)
    return jnp.concatenate(
        [jnp.where(down == lane + start, 1.0, 0.0).astype(BF16) for start in range(0, count, 128)], axis=1
    )


def turned(values, cosine, sine):
    return values * cosine + pltpu.roll(values, HD // 2, 1) * sine


def kernel(
    hidden_ref, keep_ref, picks_ref, gain_ref, wq_ref, wkv_ref, angles_ref, out_ref,
    q_all, kv_all, hidden, kept, others, outgoing, incoming, rows_all, normed, angles, q_sum, span_kv,
    send_sems, recv_sems, local_sems,
):
    me = lax.axis_index("seq")
    tp = lax.axis_index("tp")
    zl, x, y = me // (NX * NY), me // NY % NX, me % NY
    zh, core = tp // 2, tp % 2
    odd = me % 2
    spot = me % LINE
    rows = picks_ref.shape[1]
    half = rows // 2
    features = hidden_ref.shape[1]
    choices = keep_ref.shape[1]

    def device(way):
        dx, dy, dz = way
        nx, ny, nz = lax.rem(x + dx + NX, NX), lax.rem(y + dy + NY, NY), lax.rem(zl + dz, 2)
        return (nz * (NX * NY) + nx * NY + ny, tp)

    def slot(dz, other):
        return lax.rem(zh + dz + NZ, NZ) * 2 + (1 - core if other else core)

    mate = (me + 1 - 2 * odd, tp)
    sibling = (me, tp + 1 - 2 * core)
    above, below = (me, slot(1, False)), (me, slot(-1, False))
    line = [
        lax.rem(spot // 2 * 2 + 1 - spot % 2, LINE),
        lax.rem(spot + 2, LINE),
        LINE - 1 - spot,
    ]

    def at(ref, other, xo, yo):
        plane = lax.rem(zl + other, 2)
        row = lax.rem(y + yo + 2 * NY, NY)
        if xo is None:
            return ref.at[plane, :, row]
        return ref.at[plane, lax.rem(x + xo + 2 * NX, NX), row]

    loads = [
        pltpu.make_async_copy(hidden_ref, hidden, local_sems.at[0]),
        pltpu.make_async_copy(wq_ref, at(q_all, 0, 0, 0), local_sems.at[1]),
        pltpu.make_async_copy(wkv_ref, at(kv_all, 0, 0, 0), local_sems.at[2]),
        pltpu.make_async_copy(angles_ref.at[:, pl.ds(pl.multiple_of(spot * rows, rows), rows)], angles, local_sems.at[3]),
    ]
    for load in loads:
        load.start()

    barrier = pltpu.get_barrier_semaphore()
    partners = [device(way) for way in (X_RIGHT, X_LEFT, Y_RIGHT, Y_LEFT, Z_OTHER)]
    partners += [sibling, above, below] + [(me - spot + line[1], tp), (me - spot + line[2], tp)]
    for partner in partners:
        pl.semaphore_signal(barrier, inc=1, device_id=partner, device_id_type=MESH)
    pl.semaphore_wait(barrier, len(partners))

    copies = []
    table = {}

    def push(src, dst, landing, where):
        number = len(copies)
        copy = pltpu.make_async_remote_copy(
            src_ref=src, dst_ref=dst, send_sem=send_sems.at[number], recv_sem=recv_sems.at[number],
            device_id=where, device_id_type=MESH,
        )
        copy.start()
        copies.append(copy)
        return pltpu.make_async_remote_copy(
            src_ref=landing, dst_ref=landing, send_sem=send_sems.at[number], recv_sem=recv_sems.at[number],
            device_id=where, device_id_type=MESH,
        )

    def send(ref, way, other, xo, yo, src=None):
        dst = at(ref, other, xo, yo)
        dx, dy, dz = way
        there = (other + dz) % 2, None if xo is None else xo - dx, yo - dy
        table[(id(ref), way) + there] = push(dst if src is None else src, dst, at(ref, *there), device(way))

    def arrived(ref, way, other, xo, yo):
        table.pop((id(ref), way, other, xo, yo)).wait_recv()

    picks_in = push(picks_ref, others, others, mate)
    send(kv_all, Z_OTHER, 0, 0, 0, wkv_ref)
    send(q_all, Z_OTHER, 0, 0, 0, wq_ref)
    for way in (X_RIGHT, X_LEFT):
        send(kv_all, way, 0, 0, 0, wkv_ref)
    for way in (Y_RIGHT, Y_LEFT):
        send(q_all, way, 0, 0, 0, wq_ref)
    for way in (X_RIGHT, X_LEFT):
        send(q_all, way, 0, 0, 0, wq_ref)

    first_hot = one_hot(keep_ref[...], 0, hidden.shape[0])
    loads[0].wait()
    kept[...] = jnp.dot(first_hot, hidden[...], preferred_element_type=F32).astype(BF16)
    picks_in.wait_recv()
    outgoing[...] = jnp.dot(
        one_hot(others[...], odd * choices, choices), kept[...], preferred_element_type=F32
    ).astype(BF16)
    rows_in = push(outgoing, incoming, incoming, mate)

    arrived(kv_all, Z_OTHER, 1, 0, 0)
    for way in (X_RIGHT, X_LEFT):
        send(kv_all, way, 1, 0, 0)
    arrived(q_all, Z_OTHER, 1, 0, 0)
    for way in (Y_RIGHT, Y_LEFT):
        send(q_all, way, 1, 0, 0)
    for way in (X_RIGHT, X_LEFT):
        send(q_all, way, 1, 0, 0)
    own_rows = jnp.dot(
        one_hot(picks_ref[...], odd * choices, choices), kept[...], preferred_element_type=F32
    ).astype(BF16)
    rows_all[tp] = own_rows
    arrived(kv_all, X_RIGHT, 0, -1, 0)
    send(kv_all, X_RIGHT, 0, -1, 0)
    arrived(kv_all, X_LEFT, 1, 1, 0)
    send(kv_all, X_LEFT, 1, 1, 0)
    arrived(kv_all, X_LEFT, 0, 1, 0)
    arrived(kv_all, X_RIGHT, 1, -1, 0)
    loads[2].wait()

    def second_hop(yo):
        arrived(q_all, X_RIGHT, 0, -1, yo)
        send(q_all, X_RIGHT, 0, -1, yo)
        arrived(q_all, X_LEFT, 1, 1, yo)
        send(q_all, X_LEFT, 1, 1, yo)

    def kv_hop(step):
        if step == 0:
            arrived(kv_all, X_RIGHT, 0, -2, 0)
            arrived(kv_all, X_LEFT, 1, 2, 0)
            for way in (Y_RIGHT, Y_LEFT):
                for other in (0, 1):
                    send(kv_all, way, other, None, 0)
            return
        for other in (0, 1):
            for way, sign, far in ((Y_RIGHT, -1, 4 - other), (Y_LEFT, 1, 3 + other)):
                if step <= far:
                    arrived(kv_all, way, other, None, sign * step)
                    if step < far:
                        send(kv_all, way, other, None, sign * step)

    def q_hop(step):
        for other in (0, 1):
            for way, sign, far in ((Y_RIGHT, -1, 4 - other), (Y_LEFT, 1, 3 + other)):
                if step <= far:
                    arrived(q_all, way, other, 0, sign * step)
                    if step < far:
                        send(q_all, way, other, 0, sign * step)
                    for side in (X_RIGHT, X_LEFT):
                        send(q_all, side, other, 0, sign * step)

    def block(dz, other, part=None):
        ref = rows_all.at[slot(dz, other)]
        if part is None:
            return ref
        return ref.at[pl.ds(part * half, half)]

    q_hop(1)
    kv_hop(0)
    rows_in.wait_recv()
    rows_all[tp] = rows_all[tp] + incoming[...]
    mine = block(0, False)
    to_above = push(mine, mine, block(-1, False), above)
    to_below = push(mine, mine, block(1, False), below)
    crossed = [push(mine, mine, block(0, True), sibling)]
    second_hop(0)
    q_hop(2)
    second_hop(-1)
    second_hop(1)
    kv_hop(1)
    q_hop(3)
    second_hop(-2)
    to_above.wait_recv()
    far_above = push(block(-1, False, 0), block(-1, False, 0), block(2, False, 0), above)
    to_below.wait_recv()
    far_below = push(block(1, False, 1), block(1, False, 1), block(2, False, 1), below)
    crossed.append(push(block(-1, False), block(-1, False), block(-1, True), sibling))
    crossed.append(push(block(1, False), block(1, False), block(1, True), sibling))
    kv_hop(2)
    second_hop(2)
    for other, way, sign in ((0, Y_RIGHT, -1), (1, Y_LEFT, 1)):
        arrived(q_all, way, other, 0, sign * 4)
        for side in (X_RIGHT, X_LEFT):
            send(q_all, side, other, 0, sign * 4)
    second_hop(-3)
    far_above.wait_recv()
    far_below.wait_recv()
    crossed.append(push(block(2, False), block(2, False), block(2, True), sibling))
    kv_hop(3)
    second_hop(3)
    arrived(q_all, X_RIGHT, 0, -1, -4)
    send(q_all, X_RIGHT, 0, -1, -4)
    arrived(q_all, X_LEFT, 1, 1, 4)
    send(q_all, X_LEFT, 1, 1, 4)

    for copy in crossed:
        copy.wait_recv()
    squares = jnp.zeros((rows, 128), F32)
    for t in range(NT):
        wide = rows_all[t].astype(F32)
        wide = wide * wide
        for start in range(0, features, 128):
            squares = squares + wide[:, start:start + 128]
    inverse = lax.rsqrt(jnp.sum(squares, axis=1, keepdims=True) / (NT * features) + eps)
    for t in range(NT):
        normed[t] = (
            rows_all[t].astype(F32) * inverse * gain_ref[0:1, t * features:(t + 1) * features]
        ).astype(BF16)

    loads[3].wait()
    cosine, sine = angles[0], angles[1]
    kv_hop(4)
    kv_cols = kv_all.shape[-1]

    def kv_part(t, total):
        weights = kv_all[t // NX, t % NX].reshape(features, kv_cols)
        return total + jnp.dot(normed[t], weights, preferred_element_type=F32)

    keyval = lax.fori_loop(0, NT, kv_part, jnp.zeros((rows, kv_cols), F32))
    span_kv[spot] = jnp.concatenate(
        [turned(keyval[:, :HD], cosine, sine), keyval[:, HD:]], axis=1
    ).astype(BF16)
    shared = [
        push(span_kv.at[spot], span_kv.at[spot], span_kv.at[place], (me - spot + place, tp))
        for place in line
    ]

    loads[1].wait()
    q_sum[...] = jnp.zeros_like(q_sum)

    def q_part(yo):
        low = 1 if yo < -3 else 0
        for other in (0, 1):
            off = 4 if low and other else yo
            for way, xo in ((X_RIGHT, -1), (X_LEFT, 1), (X_RIGHT if other == 0 else X_LEFT, -2 if other == 0 else 2)):
                key = (id(q_all), way, other, xo, off)
                if key in table:
                    arrived(q_all, way, other, xo, off)
        row = lax.rem(y + yo + NY, NY)
        depth = q_all.shape[3]
        columns = pl.ds(pl.multiple_of(row * depth, depth), depth)

        def add(xx, carry):
            q_sum[...] += jnp.dot(
                normed[xx, :, columns], q_all[0, xx, row], preferred_element_type=F32
            ) + jnp.dot(normed[NX + xx, :, columns], q_all[1, xx, row], preferred_element_type=F32)
            return carry

        lax.fori_loop(0, NX, add, 0)

    for yo in (0, -1, 1, -2, 2, -3, 3, -4):
        q_part(yo)

    for copy in shared:
        copy.wait_recv()
    span = LINE * rows
    keys = span_kv[:, :, :HD].reshape(span, HD)
    values = span_kv[:, :, HD:].reshape(span, HD)
    position = lax.broadcasted_iota(jnp.int32, (rows, span), 0) + spot * rows
    causal = position >= lax.broadcasted_iota(jnp.int32, (rows, span), 1)
    factor = math.log2(math.e) / math.sqrt(HD)
    for head in range(q_sum.shape[1] // HD):
        lanes = slice(head * HD, (head + 1) * HD)
        rot_query = turned(q_sum[:, lanes], cosine, sine).astype(BF16)
        scores = lax.dot_general(rot_query, keys, (((1,), (1,)), ((), ())), preferred_element_type=F32)
        scores = jnp.where(causal, scores, -jnp.inf)
        weights = jnp.exp2((scores - jnp.max(scores, axis=1, keepdims=True)) * factor)
        weights = (weights * (1.0 / jnp.sum(weights, axis=1, keepdims=True))).astype(BF16)
        out_ref[:, lanes] = jnp.dot(weights, values, preferred_element_type=F32).astype(BF16)

    assert not table
    for copy in copies:
        copy.wait_send()


def local(angles, hidden, keep_first, keep_second, norm_gain, w_query, w_keyval):
    rows = keep_second.shape[0]
    depth, q_cols = w_query.shape
    kv_cols = 2 * w_keyval.shape[2]
    span, features = hidden.shape
    choices = keep_first.shape[1]
    vmem = pl.BlockSpec(memory_space=pltpu.VMEM)
    away = pl.BlockSpec(memory_space=pl.ANY)
    return pl.pallas_call(
        kernel,
        out_shape=jax.ShapeDtypeStruct((rows, q_cols), BF16),
        in_specs=[away, vmem, vmem, vmem, away, away, away],
        out_specs=vmem,
        scratch_shapes=[
            pltpu.VMEM((2, NX, NY, depth, q_cols), BF16),
            pltpu.VMEM((2, NX, NY, depth, kv_cols), BF16),
            pltpu.VMEM((span, features), BF16),
            pltpu.VMEM((choices, features), BF16),
            pltpu.VMEM((1, rows), jnp.int32),
            pltpu.VMEM((rows, features), BF16),
            pltpu.VMEM((rows, features), BF16),
            pltpu.VMEM((NT, rows, features), BF16),
            pltpu.VMEM((NT, rows, features), BF16),
            pltpu.VMEM((2, rows, HD), F32),
            pltpu.VMEM((rows, q_cols), F32),
            pltpu.VMEM((LINE, rows, kv_cols), BF16),
            pltpu.SemaphoreType.DMA((COPIES,)),
            pltpu.SemaphoreType.DMA((COPIES,)),
            pltpu.SemaphoreType.DMA((4,)),
        ],
        compiler_params=pltpu.CompilerParams(
            collective_id=0, has_side_effects=True, vmem_limit_bytes=56 * 1024 * 1024
        ),
        cost_estimate=pl.CostEstimate(flops=7_000_000_000, bytes_accessed=20_000_000, transcendentals=1_000_000),
    )(
        hidden, keep_first, keep_second.reshape(1, rows), norm_gain.reshape(1, -1), w_query,
        w_keyval.reshape(depth, kv_cols), angles,
    )


def rotary_tables(length):
    spread = np.exp(np.arange(HD // 2, dtype=np.float32) * np.float32(-2.0 * math.log(10000.0) / HD))
    turn = np.arange(length, dtype=np.float32)[:, None] * spread.astype(np.float32)[None, :]
    cosine, sine = np.cos(turn.astype(np.float64)), np.sin(turn.astype(np.float64))
    return np.stack(
        [np.concatenate([cosine, cosine], axis=1), np.concatenate([-sine, sine], axis=1)]
    ).astype(np.float32)


def solution(mesh):
    placed = (P("seq", "tp"), P("seq", None), P("seq"), P(), P("seq", "tp"), P("seq", None, "tp"))
    tables = rotary_tables(1024)

    def run(*args):
        return jax.shard_map(
            local, mesh=mesh, in_specs=(P(),) + placed, out_specs=P("seq", "tp"), check_vma=False
        )(jnp.asarray(tables), *args)

    return run
```

time: 169 us -> 107 us (0.63)
  the two profiles are of different devices: /device:TPU:256 before, /device:TPU:14 now
where the time goes in v2:
time: 107 us
  Pallas kernels  104 us (97%)
  local copies, waits for them, and re-layouts  3.15 us (3%)
    pallas_call x1, Pallas kernels, local(): pl.pallas_call(kernel, out_shape=jax.ShapeDtypeStruct((rows, q_cols), BF1...  104 us
    unnamed x2, local copies, waits for them, and re-layouts  3.15 us

profile of v2, /device:TPU:14, one launch (start us, length us, event | category | flops | bytes accessed | tf_op | source)
XLA Modules:
  0.0 106.7 jit_solution(6078170383060122131)
XLA Ops:
  0.0 1.5 %copy.10 = bf16[16,8,2,128]{3,1,2,0:T(8,128)(2,1)} copy(bf16[16,8,2,128]{3,2,1,0:T(2,128)(2,1)} %bitcast.6) | data formatting | bytes 131072
  1.5 103.5 %shard_map.73 = bf16[256,512]{1,0:T(8,128)(2,1)} custom-call(bf16[1024,1024]{1,0:T(8,128)(2,1)} %hidden_ref.1, s32[1,512]{1,0:T(1,128)} %keep_ref.1, s32[1,256]{1,0:T(1,128)} %bitcast.9, f32[1,8192]{1,0:T(1,128)} %bitcast.8, bf16[128,512]{1,0:T(8,128)(2,1)} %wq_ref.1, bf16[128,256]{1,0:T(8,128)(2,1)} %bitcast.7, f32[2,1024,128]{2,1,0:T(8,128)} %constant.2.clone.angles_ref), custom_call_target="tpu_custom_call" | custom-call | flops 7000000000 | bytes 20000000 | tf_op jit(solution)/shard_map/pallas_call | solution.py:320
  105.0 1.7 %copy.12 = bf16[256,512]{1,0:T(8,128)(2,1)} copy(bf16[256,512]{1,0:T(8,128)(2,1)} %shard_map.73) | data formatting | bytes 524288

commit v3 on v2

--- a/solution.py
+++ b/solution.py
@@ -35,8 +35,8 @@
 
 
 def kernel(
-    hidden_ref, keep_ref, picks_ref, gain_ref, wq_ref, wkv_ref, angles_ref, out_ref,
-    q_all, kv_all, hidden, kept, others, outgoing, incoming, rows_all, normed, angles, q_sum, span_kv,
+    hidden_ref, keep_ref, picks_ref, gain_ref, wq_ref, wkv_in, angles_ref, out_ref,
+    wkv_ref, q_all, kv_all, hidden, kept, others, outgoing, incoming, rows_all, normed, angles, q_sum, span_kv,
     send_sems, recv_sems, local_sems,
 ):
     me = lax.axis_index("seq")
@@ -74,6 +74,7 @@
             return ref.at[plane, :, row]
         return ref.at[plane, lax.rem(x + xo + 2 * NX, NX), row]
 
+    wkv_ref[...] = jnp.concatenate([wkv_in[:, 0, :], wkv_in[:, 1, :]], axis=1)
     loads = [
         pltpu.make_async_copy(hidden_ref, hidden, local_sems.at[0]),
         pltpu.make_async_copy(wq_ref, at(q_all, 0, 0, 0), local_sems.at[1]),
@@ -320,9 +321,10 @@
     return pl.pallas_call(
         kernel,
         out_shape=jax.ShapeDtypeStruct((rows, q_cols), BF16),
-        in_specs=[away, vmem, vmem, vmem, away, away, away],
+        in_specs=[away, vmem, vmem, vmem, away, vmem, away],
         out_specs=vmem,
         scratch_shapes=[
+            pltpu.VMEM((depth, kv_cols), BF16),
             pltpu.VMEM((2, NX, NY, depth, q_cols), BF16),
             pltpu.VMEM((2, NX, NY, depth, kv_cols), BF16),
             pltpu.VMEM((span, features), BF16),
@@ -345,7 +347,7 @@
         cost_estimate=pl.CostEstimate(flops=7_000_000_000, bytes_accessed=20_000_000, transcendentals=1_000_000),
     )(
         hidden, keep_first, keep_second.reshape(1, rows), norm_gain.reshape(1, -1), w_query,
-        w_keyval.reshape(depth, kv_cols), angles,
+        w_keyval, angles,
     )
 
 

time: 107 us -> 106 us (level)
  the two profiles are of different devices: /device:TPU:14 before, /device:TPU:12 now
where the time goes in v3:
time: 106 us
  Pallas kernels  104 us (98%)
  local copies, waits for them, and re-layouts  1.67 us (2%)
    pallas_call x1, Pallas kernels, local(): pl.pallas_call(kernel, out_shape=jax.ShapeDtypeStruct((rows, q_cols), BF1...  104 us

profile of v3, /device:TPU:12, one launch (start us, length us, event | category | flops | bytes accessed | tf_op | source)
XLA Modules:
  0.0 105.6 jit_solution(14242711280909511799)
XLA Ops:
  0.0 103.9 %shard_map.73 = bf16[256,512]{1,0:T(8,128)(2,1)} custom-call(bf16[1024,1024]{1,0:T(8,128)(2,1)} %hidden_ref.1, s32[1,512]{1,0:T(1,128)} %keep_ref.1, s32[1,256]{1,0:T(1,128)} %bitcast.3, f32[1,8192]{1,0:T(1,128)} %bitcast.2, bf16[128,512]{1,0:T(8,128)(2,1)} %wq_ref.1, bf16[128,2,128]{2,1,0:T(2,128)(2,1)} %wkv_in.1, f32[2,1024,128]{2,1,0:T(8,128)} %constant.2.clone.angles_ref), custom_call_target="tpu_custom_call" | custom-call | flops 7000000000 | bytes 20000000 | tf_op jit(solution)/shard_map/pallas_call | solution.py:321
  103.9 1.7 %copy.9 = bf16[256,512]{1,0:T(8,128)(2,1)} copy(bf16[256,512]{1,0:T(8,128)(2,1)} %shard_map.73) | data formatting | bytes 524288

commit v4 on v3

--- a/solution.py
+++ b/solution.py
@@ -36,7 +36,7 @@
 
 def kernel(
     hidden_ref, keep_ref, picks_ref, gain_ref, wq_ref, wkv_in, angles_ref, out_ref,
-    wkv_ref, q_all, kv_all, hidden, kept, others, outgoing, incoming, rows_all, normed, angles, q_sum, span_kv,
+    wkv_ref, q_all, kv_all, hidden, kept, others, outgoing, incoming, rows_all, normed, angles, q_sum, early, span_kv,
     send_sems, recv_sems, local_sems,
 ):
     me = lax.axis_index("seq")
@@ -246,14 +246,23 @@
 
     loads[3].wait()
     cosine, sine = angles[0], angles[1]
+    depth = q_all.shape[3]
+
+    def kv_part(yos, total):
+        def add(xx, total):
+            for yo in yos:
+                row = lax.rem(y + yo + NY, NY)
+                columns = pl.ds(pl.multiple_of(row * depth, depth), depth)
+                total = total + jnp.dot(
+                    normed[xx, :, columns], kv_all[0, xx, row], preferred_element_type=F32
+                ) + jnp.dot(normed[NX + xx, :, columns], kv_all[1, xx, row], preferred_element_type=F32)
+            return total
+
+        return lax.fori_loop(0, NX, add, total)
+
+    early[...] = kv_part((0, -1, 1, -2, 2, -3, 3), jnp.zeros((rows, kv_all.shape[-1]), F32))
     kv_hop(4)
-    kv_cols = kv_all.shape[-1]
-
-    def kv_part(t, total):
-        weights = kv_all[t // NX, t % NX].reshape(features, kv_cols)
-        return total + jnp.dot(normed[t], weights, preferred_element_type=F32)
-
-    keyval = lax.fori_loop(0, NT, kv_part, jnp.zeros((rows, kv_cols), F32))
+    keyval = kv_part((-4,), early[...])
     span_kv[spot] = jnp.concatenate(
         [turned(keyval[:, :HD], cosine, sine), keyval[:, HD:]], axis=1
     ).astype(BF16)
@@ -274,7 +283,6 @@
                 if key in table:
                     arrived(q_all, way, other, xo, off)
         row = lax.rem(y + yo + NY, NY)
-        depth = q_all.shape[3]
         columns = pl.ds(pl.multiple_of(row * depth, depth), depth)
 
         def add(xx, carry):
@@ -336,6 +344,7 @@
             pltpu.VMEM((NT, rows, features), BF16),
             pltpu.VMEM((2, rows, HD), F32),
             pltpu.VMEM((rows, q_cols), F32),
+            pltpu.VMEM((rows, kv_cols), F32),
             pltpu.VMEM((LINE, rows, kv_cols), BF16),
             pltpu.SemaphoreType.DMA((COPIES,)),
             pltpu.SemaphoreType.DMA((COPIES,)),

time: 106 us -> 105 us (level)
  the two profiles are of different devices: /device:TPU:12 before, /device:TPU:58 now
where the time goes in v4:
time: 105 us
  Pallas kernels  103 us (98%)
  local copies, waits for them, and re-layouts  1.67 us (2%)
    pallas_call x1, Pallas kernels, local(): pl.pallas_call(kernel, out_shape=jax.ShapeDtypeStruct((rows, q_cols), BF1...  103 us

profile of v4, /device:TPU:58, one launch (start us, length us, event | category | flops | bytes accessed | tf_op | source)
XLA Modules:
  0.0 104.5 jit_solution(4551539647433049554)
XLA Ops:
  0.0 102.9 %shard_map.73 = bf16[256,512]{1,0:T(8,128)(2,1)} custom-call(bf16[1024,1024]{1,0:T(8,128)(2,1)} %hidden_ref.1, s32[1,512]{1,0:T(1,128)} %keep_ref.1, s32[1,256]{1,0:T(1,128)} %bitcast.3, f32[1,8192]{1,0:T(1,128)} %bitcast.2, bf16[128,512]{1,0:T(8,128)(2,1)} %wq_ref.1, bf16[128,2,128]{2,1,0:T(2,128)(2,1)} %wkv_in.1, f32[2,1024,128]{2,1,0:T(8,128)} %constant.2.clone.angles_ref), custom_call_target="tpu_custom_call" | custom-call | flops 7000000000 | bytes 20000000 | tf_op jit(solution)/shard_map/pallas_call | solution.py:329
  102.9 1.7 %copy.9 = bf16[256,512]{1,0:T(8,128)(2,1)} copy(bf16[256,512]{1,0:T(8,128)(2,1)} %shard_map.73) | data formatting | bytes 524288

commit v5 on v4

--- a/solution.py
+++ b/solution.py
@@ -282,19 +282,24 @@
                 key = (id(q_all), way, other, xo, off)
                 if key in table:
                     arrived(q_all, way, other, xo, off)
-        row = lax.rem(y + yo + NY, NY)
-        columns = pl.ds(pl.multiple_of(row * depth, depth), depth)
-
-        def add(xx, carry):
-            q_sum[...] += jnp.dot(
-                normed[xx, :, columns], q_all[0, xx, row], preferred_element_type=F32
-            ) + jnp.dot(normed[NX + xx, :, columns], q_all[1, xx, row], preferred_element_type=F32)
-            return carry
-
-        lax.fori_loop(0, NX, add, 0)
-
-    for yo in (0, -1, 1, -2, 2, -3, 3, -4):
-        q_part(yo)
+
+    def q_rows(yos):
+        for yo in yos:
+            q_part(yo)
+
+        def add(xx, total):
+            for yo in yos:
+                row = lax.rem(y + yo + NY, NY)
+                columns = pl.ds(pl.multiple_of(row * depth, depth), depth)
+                total = total + jnp.dot(
+                    normed[xx, :, columns], q_all[0, xx, row], preferred_element_type=F32
+                ) + jnp.dot(normed[NX + xx, :, columns], q_all[1, xx, row], preferred_element_type=F32)
+            return total
+
+        q_sum[...] = lax.fori_loop(0, NX, add, q_sum[...])
+
+    q_rows((0, -1, 1, -2, 2, -3))
+    q_rows((3, -4))
 
     for copy in shared:
         copy.wait_recv()

time: 105 us -> 104 us (level)
  the two profiles are of different devices: /device:TPU:58 before, /device:TPU:12 now
where the time goes in v5:
time: 104 us
  Pallas kernels  102 us (98%)
  local copies, waits for them, and re-layouts  1.67 us (2%)
    pallas_call x1, Pallas kernels, local(): pl.pallas_call(kernel, out_shape=jax.ShapeDtypeStruct((rows, q_cols), BF1...  102 us

profile of v5, /device:TPU:12, one launch (start us, length us, event | category | flops | bytes accessed | tf_op | source)
XLA Modules:
  0.0 104.1 jit_solution(1999819079391466432)
XLA Ops:
  0.0 102.4 %shard_map.73 = bf16[256,512]{1,0:T(8,128)(2,1)} custom-call(bf16[1024,1024]{1,0:T(8,128)(2,1)} %hidden_ref.1, s32[1,512]{1,0:T(1,128)} %keep_ref.1, s32[1,256]{1,0:T(1,128)} %bitcast.3, f32[1,8192]{1,0:T(1,128)} %bitcast.2, bf16[128,512]{1,0:T(8,128)(2,1)} %wq_ref.1, bf16[128,2,128]{2,1,0:T(2,128)(2,1)} %wkv_in.1, f32[2,1024,128]{2,1,0:T(8,128)} %constant.2.clone.angles_ref), custom_call_target="tpu_custom_call" | custom-call | flops 7000000000 | bytes 20000000 | tf_op jit(solution)/shard_map/pallas_call | solution.py:334
  102.5 1.7 %copy.9 = bf16[256,512]{1,0:T(8,128)(2,1)} copy(bf16[256,512]{1,0:T(8,128)(2,1)} %shard_map.73) | data formatting | bytes 524288
